TPU v7x, 512 devices: a whole 4x8x8 slice. The times are simulated.
512 devices in a mesh: rows: 64 (over z, x, core), heads: 8 (over y).
Axes of the slice: x: 4, y: 8, z: 8, core: 2. Of those that a mesh axis runs over, the one named last changes fastest.
Arguments:
- queries: bfloat16 [1024, 6144], P('rows', 'heads'), may hold values from -8 to 8
- keys: bfloat16 [65536, 6144], P('rows', 'heads'), may hold values from -8 to 8
- values: bfloat16 [65536, 6144], P('rows', 'heads'), may hold values from -6 to 6
- pattern: int32 [8, 16], replicated, may hold values from 0 to 63, all different within a row; in each aligned block of 8 rows (0 to 7, 8 to 15, ...) at most 4 rows name the same one
- out_weight: bfloat16 [6144, 6144], P('heads', 'rows'), may hold values from -0.5 to 0.5
Outputs:
- projected: bfloat16 [1024, 6144], P('heads', 'rows')
Inputs may be any that keep to these rules, and one draw needn't show every extreme that they name: `pattern`: each row names 16 different cache blocks; no cache block is named by more than 4 rows, one by exactly 4; every cache block is named by some row.
All inputs are finite; a program needn't handle non-finite values.
Results may differ from a plain program's by a relative error of at most 0.0051.
Values may be sent and summed in bfloat16 or wider, within the bound.
A program may use at most 64 MiB of HBM per device.

v0:
```python
import jax
import jax.numpy as jnp
from jax import lax
from jax.sharding import PartitionSpec as P

HD = 128


NEG_FILL = -1e30


def block_partial(query_block, key_heads, value_heads):
    head_count = key_heads.shape[1]
    query_heads = query_block.reshape(query_block.shape[0], head_count, key_heads.shape[2])
    scores = jnp.einsum(
        "qhd,khd->hqk", query_heads, key_heads, preferred_element_type=jnp.float32
    ) * key_heads.shape[2] ** (-0.5)
    row_max = jnp.max(scores, axis=2)
    exp_scores = jnp.exp(scores - row_max[:, :, None])
    row_total = jnp.sum(exp_scores, axis=2)
    weights = exp_scores.astype(jnp.bfloat16)
    mixed_out = jnp.einsum("hqk,khd->qhd", weights, value_heads, preferred_element_type=jnp.float32)
    normed = mixed_out / row_total.T[:, :, None]
    return (normed.reshape(query_block.shape[0], -1), (row_max + jnp.log(row_total)).T)


def merge_home(received):
    got_out, got_lse = received
    sources, items, head_count = got_lse.shape
    row_max = jnp.max(got_lse, axis=0)
    factor = jnp.exp(got_lse - row_max[None])
    spread = got_out.reshape(sources, items, head_count, -1)
    numerator = jnp.sum(factor[..., None] * spread, axis=0)
    denominator = jnp.sum(factor, axis=0)
    return (numerator / denominator[..., None]).reshape(items, -1).astype(jnp.bfloat16)


def spread_merge(
    linked,
    row_count,
    pattern,
    every_query,
    block_len,
    key_heads,
    value_heads,
    width_here,
    head_count,
    all_tokens,
    own_tokens,
    project,
):
    block_count = pattern.shape[0]
    query_blocks = every_query.reshape(block_count, block_len, width_here)
    block_out, block_lse = lax.map(
        lambda query_block: block_partial(query_block, key_heads, value_heads), query_blocks
    )
    full_out = block_out.reshape(all_tokens, width_here)
    full_lse = jnp.where(linked[:, None, None], block_lse, NEG_FILL).reshape(all_tokens, head_count)
    send_out = full_out.reshape(row_count, own_tokens, width_here)
    send_lse = full_lse.reshape(row_count, own_tokens, head_count)
    attended = merge_home(
        (
            lax.all_to_all(send_out, "rows", split_axis=0, concat_axis=0, tiled=True),
            lax.all_to_all(send_lse, "rows", split_axis=0, concat_axis=0, tiled=True),
        )
    )
    projected = project(lax.all_gather(attended, "rows", axis=0, tiled=True), jnp.int32(0))
    return projected


def shards(queries, keys, values, pattern, out_weight):
    row_count = lax.axis_size("rows")
    every_query = lax.all_gather(queries, "rows", axis=0, tiled=True)
    own_block = lax.axis_index("rows")
    width_here = keys.shape[1]
    head_count = width_here // HD
    key_heads = keys.reshape(keys.shape[0], head_count, HD)
    value_heads = values.reshape(values.shape[0], head_count, HD)
    block_count = pattern.shape[0]
    all_tokens = every_query.shape[0]
    block_len = all_tokens // block_count
    own_tokens = queries.shape[0]
    linked = jnp.any(pattern == own_block, axis=1)

    def project(shard_rows, row_start):
        return jnp.dot(shard_rows, out_weight, preferred_element_type=jnp.float32)

    projected = spread_merge(
        linked,
        row_count,
        pattern,
        every_query,
        block_len,
        key_heads,
        value_heads,
        width_here,
        head_count,
        all_tokens,
        own_tokens,
        project,
    )
    return lax.psum_scatter(projected, "heads", scatter_dimension=0, tiled=True).astype(
        jnp.bfloat16
    )


def solution(mesh):
    in_specs = (P("rows", "heads"), P("rows", "heads"), P("rows", "heads"), P(), P("heads", "rows"))
    out_specs = P("heads", "rows")
    return jax.shard_map(shards, mesh=mesh, in_specs=in_specs, out_specs=out_specs, check_vma=False)
```

profile of v0, /device:TPU:1, one launch (start us, length us, event | category | flops | bytes accessed | tf_op | source)
XLA Modules:
  0.0 358.4 jit_solution(9938452570600633378)
XLA Ops:
  6.5 0.7 all-gather.3.cloned.1.call-update
  7.3 1.7 copy.34
  9.0 0.9 copy.37
  9.9 2.6 copy.35
  12.6 87.0 %all-gather.3.cloned.1.call-done = bf16[1024,768]{1,0:T(8,128)(2,1)} async-done(((bf16[16,768]{1,0:T(8,128)(2,1)}), bf16[1024,768]{1,0:T(8,128)(2,1)}) %all-gather.3.cloned.1.call-update) | async-done | bytes 1572880 | tf_op jit(solution)/shard_map/all_gather | solution.py:73
  99.7 35.3 %while.12 = (s32[]{:T(128)}, f32[8,128,768]{2,1,0:T(8,128)}, f32[8,128,6]{1,2,0:T(8,128)S(1)}, bf16[8,128,768]{2,1,0:T(8,128)(2,1)}, bf16[1024,6,128]{2,0,1:T(8,...) while((s32[]{:T(128)}, f32[8,128,768]{2,1,0:T(8,128)}, f32[8,128,6]{1,2,0:T(8,128)S(1)}, ...), condition=%wide.region_4.5_spmd, body=%wide.region_1.4_spmd.sunk | while | flops 409042176 | bytes 21851760 | solution.py:54
  99.7 0.9 constant_dynamic-slice_fusion.2
  101.5 0.7 fusion.31
  102.2 0.9 fusion.32
  103.3 0.8 constant_dynamic-update-slice_fusion.2
  104.1 0.9 constant_dynamic-slice_fusion.2
  105.9 0.7 fusion.31
  106.6 0.9 fusion.32
  107.7 0.8 constant_dynamic-update-slice_fusion.2
  108.4 0.9 constant_dynamic-slice_fusion.2
  110.3 0.7 fusion.31
  111.0 0.9 fusion.32
  112.1 0.8 constant_dynamic-update-slice_fusion.2
  112.9 0.9 constant_dynamic-slice_fusion.2
  114.7 0.7 fusion.31
  115.4 0.9 fusion.32
  116.5 0.8 constant_dynamic-update-slice_fusion.2
  117.3 0.9 constant_dynamic-slice_fusion.2
  119.1 0.7 fusion.31
  119.9 0.9 fusion.32
  120.9 0.8 constant_dynamic-update-slice_fusion.2
  121.8 0.9 constant_dynamic-slice_fusion.2
  123.6 0.7 fusion.31
  124.3 0.9 fusion.32
  125.4 0.8 constant_dynamic-update-slice_fusion.2
  126.2 0.9 constant_dynamic-slice_fusion.2
  128.0 0.7 fusion.31
  128.7 0.9 fusion.32
  129.8 0.8 constant_dynamic-update-slice_fusion.2
  130.6 0.9 constant_dynamic-slice_fusion.2
  132.4 0.7 fusion.31
  133.1 0.9 fusion.32
  134.2 0.8 constant_dynamic-update-slice_fusion.2
  135.3 19.5 %all_to_all.10 = f32[64,16,6]{1,2,0:T(8,128)S(1)} all-to-all(f32[64,16,6]{1,2,0:T(8,128)S(1)} %copy.39), channel_id=1, replica_groups=mesh['rows'=64,'heads'=8] {'rows'}, dimensions={0} | all-to-all | bytes 49152 | tf_op jit(solution)/shard_map/all_to_all | solution.py:64
  154.9 5.2 %all-to-all-start.1 = ((f32[64,16,768]{2,1,0:T(8,128)}), f32[64,16,768]{2,1,0:T(8,128)}, u32[]{:S(2)}, u32[]{:S(2)}) async-start(f32[64,16,768]{2,1,0:T(8,128)} %bitcast.53), calls=%async_computation.1 | async-start | bytes 6291456 | tf_op jit(solution)/shard_map/all_to_all | solution.py:63
  160.9 2.6 mul.14
  163.4 3.2 mul.15
  166.7 66.2 %all-to-all-done.1 = f32[64,16,768]{2,1,0:T(8,128)} async-done(((f32[64,16,768]{2,1,0:T(8,128)}), f32[64,16,768]{2,1,0:T(8,128)}, u32[]{:S(2)}, u32[]{:S(2)}) %all-to-all-start.1) | async-done | bytes 3145760 | tf_op jit(solution)/shard_map/all_to_all | solution.py:63
  232.8 2.2 multiply_reduce_fusion.1
  235.8 80.4 %all-gather.5.cloned.1.call-done = bf16[1024,768]{1,0:T(8,128)(2,1)} async-done(((bf16[16,768]{1,0:T(8,128)(2,1)}), bf16[1024,768]{1,0:T(8,128)(2,1)}) %all-gather.5.cloned.1.call-update) | async-done | bytes 1572880 | tf_op jit(solution)/shard_map/all_gather | solution.py:67
  316.2 2.8 fusion.15
  319.0 31.4 %reduce-scatter.2.cloned.1.call-done = f32[128,96]{0,1:T(8,128)} async-done(((f32[1024,96]{0,1:T(8,128)}), f32[128,96]{0,1:T(8,128)}) %reduce-scatter.2.cloned.1.call-update) | async-done | bytes 49168 | tf_op jit(solution)/shard_map/reduce_scatter | solution.py:102
  350.4 1.4 convert_element_type.10
  (71 shorter events, 10.3 us)
Async XLA Ops:
  6.5 309.7 %copy-start = (bf16[768,96]{0,1:T(8,128)(2,1)S(1)}, bf16[768,96]{0,1:T(8,128)(2,1)}, u32[]{:S(2)}) copy-start(bf16[768,96]{0,1:T(8,128)(2,1)} %param.11) | copy-start | bytes 442372
  6.5 93.1 %all-gather.3.cloned.1.call-start = ((), (), s32[]{:S(2)}) async-start(), calls=%async_computation.3 | async-start | bytes 1597440 | tf_op jit(solution)/shard_map/all_gather | solution.py:73
  9.0 3.5 copy-start.2
  100.8 1.4 copy-start.1
  105.2 1.4 copy-start.1
  109.6 1.4 copy-start.1
  114.0 1.4 copy-start.1
  118.4 1.4 copy-start.1
  122.9 1.4 copy-start.1
  127.3 1.4 copy-start.1
  131.7 1.4 copy-start.1
  154.9 77.9 %all-to-all-start.1 = ((f32[64,16,768]{2,1,0:T(8,128)}), f32[64,16,768]{2,1,0:T(8,128)}, u32[]{:S(2)}, u32[]{:S(2)}) async-start(f32[64,16,768]{2,1,0:T(8,128)} %bitcast.53), calls=%async_computation.1 | async-start | bytes 6291456 | tf_op jit(solution)/shard_map/all_to_all | solution.py:63
  160.1 156.1 %all-gather.5.cloned.1.call-start = ((), (), s32[]{:S(2)}) async-start(), calls=%async_computation.4 | async-start | bytes 1597440 | tf_op jit(solution)/shard_map/all_gather | solution.py:67
  235.8 114.6 %reduce-scatter.2.cloned.1.call-start = ((), (), s32[]{:S(2)}) async-start(), calls=%async_computation.5 | async-start | bytes 442368 | tf_op jit(solution)/shard_map/reduce_scatter | solution.py:102
Sparse Core Ops, SparseCore 0:
  10.7 88.9 all-gather.2
  235.9 80.2 all-gather.4
  319.1 31.2 reduce-scatter.1
where the time goes:
time: 363 us; the launch traced here: 358 us
  waiting for transfers between devices  266 us (73%)
  local copies, waits for them, and re-layouts  28.3 us (8%)
  blocking collectives  19.5 us (5%)
  matrix products  15.4 us (4%)
  between operations  13.2 us (4%)
  other arithmetic  10.5 us (3%)
  starting transfers between devices  5.31 us (1%)
    all_gather x1, waiting for transfers between devices, shards(): every_query = lax.all_gather(queries, 'rows', axis=0, tiled=True)  87 us
    all_gather x1, waiting for transfers between devices, spread_merge(): lax.all_gather(attended, 'rows', axis=0, tiled=True)  80.4 us
    all_to_all x1, waiting for transfers between devices, spread_merge(): lax.all_to_all(send_out, 'rows', split_axis=0, concat_axis=0, tiled=True)  66.2 us
    reduce_scatter x1, waiting for transfers between devices, shards(): lax.psum_scatter(projected, 'heads', scatter_dimension=0, tiled=True)  31.4 us
    all_to_all x1, blocking collectives, spread_merge(): lax.all_to_all(send_lse, 'rows', split_axis=0, concat_axis=0, tiled=True)  19.5 us
    dynamic_slice x16, local copies, waits for them, and re-layouts, spread_merge(): lax.map(lambda query_block: block_partial(query_block, key_heads, value_h...  8.83 us
    dynamic_update_slice x16, local copies, waits for them, and re-layouts, spread_merge(): lax.map(lambda query_block: block_partial(query_block, key_heads, value_h...  7.67 us
  transfers between devices with their start and end apart: 4, of which 4 were waited for; matrix products, arithmetic and copies ran while one was open for 3% of the time, Pallas kernels for 0%

commit v1 on v0

v1 whole, which is shorter than its diff:
```python
import functools
import math

import jax
import jax.numpy as jnp
from jax import lax
from jax.experimental import pallas as pl
from jax.experimental.pallas import tpu as pltpu
from jax.sharding import PartitionSpec as P

MESH = pl.DeviceIdType.MESH
HD = 128
QB = 128
MOST = 4
CORES = 2
XN = 4
STATS = 16
LOW = -(2.0**100)
NT = (((1,), (1,)), ((), ()))
BF = jnp.bfloat16
F32 = jnp.float32


def near_first(n):
    order = []
    for step in range(1, n // 2 + 1):
        order.append(step)
        if n - step != step:
            order.append(n - step)
    return order


def kernel(
    q_ref,
    k_ref,
    v_ref,
    pat_ref,
    w_ref,
    out_ref,
    q_all,
    k_buf,
    v_buf,
    v_t,
    w_in,
    w_t,
    w_all,
    q_sel,
    num,
    top,
    tot,
    parts,
    parts_in,
    sums,
    sums_in,
    att,
    acc,
    acc_in,
    masks,
    local_sem,
    qz_s,
    qz_r,
    qx_s,
    qx_r,
    kv_s,
    kv_r,
    w_s,
    w_r,
    rx_s,
    rx_r,
    rz_s,
    rz_r,
    az_s,
    az_r,
    ax_s,
    ax_r,
    sib_s,
    sib_r,
    ready,
):
    r = lax.axis_index("rows")
    y = lax.axis_index("heads")
    yn = w_all.shape[0]
    zn = att.shape[0]
    nb = zn
    heads = num.shape[2] // HD
    half = heads * HD
    dq = HD // XN
    body = heads * dq
    own = q_ref.shape[0]
    z = r // (XN * CORES)
    x = (r // CORES) % XN
    c = r % CORES
    sib = 1 - c

    def dev(dz, dx, dc, dy):
        return ((dz * XN + dx) * CORES + dc, dy)

    def remote(src, dst, ss, rs, to):
        return pltpu.make_async_remote_copy(
            src_ref=src, dst_ref=dst, send_sem=ss, recv_sem=rs, device_id=to, device_id_type=MESH
        )

    def mod(v, n):
        return lax.rem(v + n, n)

    def half_of(which):
        return pl.ds(pl.multiple_of(which * half, HD), half)

    def q_rows(zz, xx, cc):
        return pl.ds(pl.multiple_of((zz * XN + xx) * (CORES * own) + cc * own, own), own)

    def q_pair(zz, xx):
        return pl.ds(pl.multiple_of((zz * XN + xx) * (CORES * own), CORES * own), CORES * own)

    k_own = pltpu.make_async_copy(k_ref.at[:, half_of(c)], k_buf.at[c], local_sem.at[0])
    v_own = pltpu.make_async_copy(v_ref.at[:, half_of(c)], v_buf.at[c], local_sem.at[1])
    q_own = pltpu.make_async_copy(q_ref.at[:, half_of(c)], q_all.at[q_rows(z, x, c)], local_sem.at[2])
    w_own = pltpu.make_async_copy(w_ref, w_in, local_sem.at[3])
    q_own.start()
    w_own.start()
    v_own.start()
    k_own.start()

    bar = pltpu.get_barrier_semaphore()

    def signal(to):
        pl.semaphore_signal(bar, inc=1, device_id=to, device_id_type=MESH)

    signals = 0
    for d in reversed(near_first(zn)):
        for cc in range(CORES):
            signal(dev(mod(z + d, zn), x, cc, y))
            signals += 1
    for d in reversed(near_first(yn)):
        for cc in range(CORES):
            signal(dev(z, x, cc, mod(y + d, yn)))
            signals += 1
    for d in near_first(XN):
        signal(dev(z, mod(x + d, XN), c, y))
        signals += 1
    signal(dev(z, x, sib, y))
    signals += 1

    top[...] = jnp.zeros_like(top)
    tot[...] = jnp.zeros_like(tot)

    for cb in range(CORES):
        hit = (pat_ref[...] == (z * XN + x) * CORES + cb).astype(F32)
        linked = jnp.max(hit, axis=1, keepdims=True)
        count = jnp.zeros((1, QB), F32)
        for b in range(nb):
            this = jnp.broadcast_to(linked[b : b + 1], (1, QB))
            for j in range(MOST):
                masks[b, cb * MOST + j : cb * MOST + j + 1, :] = jnp.where(count == j, this, 0.0)
            count = count + this
    pl.semaphore_wait(bar, signals)

    q_sib = remote(q_ref.at[:, half_of(sib)], q_all.at[q_rows(z, x, c)], qz_s.at[0, 0], qz_r.at[0, 0], dev(z, x, sib, y))
    q_sib.start()
    qz = {}
    for d in near_first(zn):
        for cc in range(CORES):
            copy = remote(
                q_ref.at[:, pl.ds(cc * half, half)],
                q_all.at[q_rows(z, x, c)],
                qz_s.at[d, cc],
                qz_r.at[d, c],
                dev(mod(z + d, zn), x, cc, y),
            )
            copy.start()
            qz[d, cc] = copy
    kv = [
        remote(ref.at[:, half_of(sib)], buf.at[c], kv_s.at[i], kv_r.at[i], dev(z, x, sib, y))
        for i, (ref, buf) in enumerate(((k_ref, k_buf), (v_ref, v_buf)))
    ]
    for copy in kv:
        copy.start()
    for d in range(1, yn):
        pl.semaphore_signal(ready, inc=1, device_id=dev(z, x, c, mod(y + d, yn)), device_id_type=MESH)

    def arrived(dst, sem):
        pltpu.make_async_copy(dst, dst, sem).wait()


    qx = []
    for n, d in enumerate([0] + near_first(zn)):
        zz = mod(z - d, zn)
        if d == 0:
            q_own.wait()
            arrived(q_all.at[q_rows(z, x, sib)], qz_r.at[0, 0])
        else:
            for cc in range(CORES):
                arrived(q_all.at[q_rows(zz, x, cc)], qz_r.at[d, cc])
        for e in near_first(XN):
            copy = remote(
                q_all.at[q_pair(zz, x)],
                q_all.at[q_pair(zz, x)],
                qx_s.at[d, e],
                qx_r.at[d, e],
                dev(z, mod(x + e, XN), c, y),
            )
            copy.start()
            qx.append(copy)
        if n == 0:
            w_own.wait()
            for cc in range(CORES):
                w_t[cc] = w_in[:, cc * half : (cc + 1) * half]
            w_all[y, c] = w_t[c]
            ws = [remote(w_t.at[sib], w_all.at[y, c], w_s.at[0, sib], w_r.at[0, c], dev(z, x, sib, y))]
            ws[0].start()
            for e in near_first(yn):
                for cc in range(CORES):
                    copy = remote(w_t.at[cc], w_all.at[y, c], w_s.at[e, cc], w_r.at[e, c], dev(z, x, cc, mod(y + e, yn)))
                    copy.start()
                    ws.append(copy)
            v_own.wait()
            for h in range(heads):
                v_t[c, h * HD : (h + 1) * HD, :] = v_buf[c, :, h * HD : (h + 1) * HD].T
    k_own.wait()
    for copy in kv:
        copy.wait_recv()
    for h in range(heads):
        v_t[sib, h * HD : (h + 1) * HD, :] = v_buf[sib, :, h * HD : (h + 1) * HD].T
    for d in [0] + near_first(zn):
        zz = mod(z - d, zn)
        for e in near_first(XN):
            arrived(q_all.at[q_pair(zz, mod(x - e, XN))], qx_r.at[d, e])

    scale = HD**-0.5 * math.log2(math.e)
    def choose(i, _):
        cb = i // MOST
        j = i % MOST
        mask = [masks[b, pl.ds(i, 1), :].astype(BF) for b in range(nb)]
        rows = pl.ds(pl.multiple_of(j * QB, QB), QB)
        for h in range(heads):
            cols = slice(h * HD, (h + 1) * HD)
            picked = [mask[b] * q_all[b * QB : (b + 1) * QB, cols] for b in range(nb)]
            q_sel[cb, h, rows, :] = functools.reduce(jnp.add, picked)
        return 0

    lax.fori_loop(0, CORES * MOST, choose, 0)

    def unit(i, _):
        cb = i // heads
        h = i % heads
        cols = pl.ds(pl.multiple_of(h * HD, HD), HD)
        k_h = k_buf[cb, :, cols]
        v_h = v_t[cb, cols, :]
        for p in range(MOST // 2):
            q_p = q_sel[cb, h, p * 2 * QB : (p + 1) * 2 * QB, :]
            s = lax.dot_general(k_h, q_p, NT, preferred_element_type=F32)
            m = jnp.max(s, axis=0, keepdims=True) * scale
            e = jnp.exp2(s * scale - m)
            l = jnp.sum(e, axis=0, keepdims=True)
            o = jnp.dot(v_h, e.astype(BF), preferred_element_type=F32)
            for t in range(2):
                j = p * 2 + t
                lanes = slice(t * QB, (t + 1) * QB)
                num[cb, j, cols, :] = o[:, lanes]
                top[cb, j, pl.ds(h, 1), :] = m[:, lanes]
                tot[cb, j, pl.ds(h, 1), :] = l[:, lanes]
        return 0

    lax.fori_loop(0, CORES * heads, unit, 0)

    row = lax.broadcasted_iota(jnp.int32, (8, QB), 0)

    def stats_of(m, l):
        high = l.astype(BF).astype(F32)
        first = jnp.where(row < heads, m, pltpu.roll(high, heads, 0))
        return jnp.concatenate([first, l - high], axis=0).astype(BF)

    def read_stats(block):
        block = block.astype(F32)
        first = block[0:8]
        return first, pltpu.roll(first, 8 - heads, 0) + block[8:16]

    rx = []
    for i in range(nb):
        b = mod(z - y + i + 1 + yn, nb)
        mask = masks[b]
        tops = [jnp.where(mask[i : i + 1] > 0.5, top[i // MOST, i % MOST], LOW) for i in range(CORES * MOST)]
        m = functools.reduce(jnp.maximum, tops).astype(BF).astype(F32)
        f = [jnp.exp2(t - m) for t in tops]
        stats = stats_of(m, functools.reduce(jnp.add, [f[i] * tot[i // MOST, i % MOST] for i in range(CORES * MOST)]))
        for h in range(heads):
            for xx in range(XN):
                rows = slice(h * HD + xx * dq, h * HD + (xx + 1) * dq)
                terms = [f[i][h : h + 1] * num[i // MOST, i % MOST, rows, :] for i in range(CORES * MOST)]
                parts[xx, b, h * dq : (h + 1) * dq, :] = functools.reduce(jnp.add, terms).astype(BF)
        for xx in range(XN):
            parts[xx, b, body:, :] = stats
        for e in near_first(XN):
            to = mod(x + e, XN)
            copy = remote(parts.at[to, b], parts_in.at[e, b], rx_s.at[e, i], rx_r.at[e, i], dev(z, to, c, y))
            copy.start()
            rx.append(copy)

    def merge(blocks):
        stats = [read_stats(block[body:, :]) for block in blocks]
        m = functools.reduce(jnp.maximum, [s[0] for s in stats])
        factors = [jnp.exp2(s[0] - m) for s in stats]
        l = functools.reduce(jnp.add, [f * s[1] for f, s in zip(factors, stats)])
        sums_of = []
        for h in range(heads):
            rows = slice(h * dq, (h + 1) * dq)
            sums_of.append(
                functools.reduce(
                    jnp.add, [f[h : h + 1] * block[rows, :].astype(F32) for f, block in zip(factors, blocks)]
                )
            )
        return sums_of, m, l

    pl.semaphore_wait(ready, yn - 1)
    for i in range(nb):
        b = mod(z - y + i + 1 + yn, nb)
        for e in near_first(XN):
            arrived(parts_in.at[e, b], rx_r.at[e, i])
        merged, m, l = merge([parts.at[x, b]] + [parts_in.at[e, b] for e in near_first(XN)])
        for h in range(heads):
            sums[i, h * dq : (h + 1) * dq, :] = merged[h].astype(BF)
        sums[i, body:, :] = stats_of(m, l)
        zz = mod(z + i + 1, zn)
        here = jnp.logical_and(zz == z, b == y)

        @pl.when(here)
        def _():
            pltpu.make_async_copy(sums.at[i], sums_in.at[z], rz_r.at[z]).start()

        @pl.when(jnp.logical_not(here))
        def _():
            remote(sums.at[i], sums_in.at[z], rz_s.at[i], rz_r.at[z], dev(zz, x, c, b)).start()

    for zz in range(zn):
        arrived(sums_in.at[zz], rz_r.at[zz])
    merged, m, l = merge([sums_in.at[zz] for zz in range(zn)])
    for h in range(heads):
        att[z, x, h * dq : (h + 1) * dq, :] = (merged[h] / l[h : h + 1]).astype(BF)

    def rz_wait():
        for i in range(nb):
            b = mod(z - y + i + 1 + yn, nb)
            here = jnp.logical_and(mod(z + i + 1, zn) == z, b == y)

            @pl.when(jnp.logical_not(here))
            def _():
                remote(sums.at[i], sums_in.at[z], rz_s.at[i], rz_r.at[z], dev(z, x, c, y)).wait_send()

    az, ax = [], []
    for d in near_first(zn):
        copy = remote(att.at[z, x], att.at[z, x], az_s.at[d], az_r.at[d], dev(mod(z + d, zn), x, c, y))
        copy.start()
        az.append(copy)
    for d in [0] + near_first(zn):
        zz = mod(z - d, zn)
        if d:
            arrived(att.at[zz, x], az_r.at[d])
        for e in near_first(XN):
            copy = remote(att.at[zz, x], att.at[zz, x], ax_s.at[d, e], ax_r.at[d, e], dev(z, mod(x + e, XN), c, y))
            copy.start()
            ax.append(copy)

    arrived(w_all.at[y, sib], w_r.at[0, sib])
    for e in near_first(yn):
        for cc in range(CORES):
            arrived(w_all.at[mod(y - e, yn), cc], w_r.at[e, cc])
    total = None
    for d in [0] + near_first(zn):
        zz = mod(z - d, zn)
        for e in near_first(XN):
            arrived(att.at[zz, mod(x - e, XN)], ax_r.at[d, e])
        yy = mod(zz - y, yn)
        wide = w_all[yy].reshape(CORES * w_all.shape[2], half)
        rows = jnp.concatenate(
            [att[zz, xx, h * dq : (h + 1) * dq, :] for h in range(heads) for xx in range(XN)], axis=0
        )
        term = jnp.dot(wide, rows, preferred_element_type=F32)
        total = term if total is None else total + term
    acc[...] = total.reshape(acc.shape)
    last = remote(acc.at[sib], acc_in, sib_s, sib_r, dev(z, x, sib, y))
    last.start()
    q_sib.wait_send()
    for group in (qz.values(), qx, kv, ws, rx, az, ax):
        for copy in group:
            copy.wait_send()
    rz_wait()
    last.wait()
    out_ref[...] = (acc[c] + acc_in[...]).astype(BF)


def shards(queries, keys, values, pattern, out_weight):
    yn = lax.axis_size("heads")
    zn = lax.axis_size("rows") // (XN * CORES)
    nb = pattern.shape[0]
    own, width = queries.shape
    half = width // CORES
    heads = half // HD
    cblk = keys.shape[0]
    cols = out_weight.shape[1]
    piece = heads * (HD // XN)
    load = piece + STATS
    dma = pltpu.SemaphoreType.DMA
    anywhere = pl.BlockSpec(memory_space=pl.ANY)
    return pl.pallas_call(
        kernel,
        name="attend_project",
        out_shape=jax.ShapeDtypeStruct((cols, QB), BF),
        in_specs=[anywhere, anywhere, anywhere, pl.BlockSpec(memory_space=pltpu.VMEM), anywhere],
        out_specs=pl.BlockSpec(memory_space=pltpu.VMEM),
        scratch_shapes=[
            pltpu.VMEM((nb * QB, half), BF),
            pltpu.VMEM((CORES, cblk, half), BF),
            pltpu.VMEM((CORES, cblk, half), BF),
            pltpu.VMEM((CORES, half, cblk), BF),
            pltpu.VMEM((cols, width), BF),
            pltpu.VMEM((CORES, cols, half), BF),
            pltpu.VMEM((yn, CORES, cols, half), BF),
            pltpu.VMEM((CORES, heads, MOST * QB, HD), BF),
            pltpu.VMEM((CORES, MOST, half, QB), F32),
            pltpu.VMEM((CORES, MOST, 8, QB), F32),
            pltpu.VMEM((CORES, MOST, 8, QB), F32),
            pltpu.VMEM((XN, nb, load, QB), BF),
            pltpu.VMEM((XN, nb, load, QB), BF),
            pltpu.VMEM((nb, load, QB), BF),
            pltpu.VMEM((zn, load, QB), BF),
            pltpu.VMEM((zn, XN, piece, QB), BF),
            pltpu.VMEM((CORES, cols, QB), F32),
            pltpu.VMEM((cols, QB), F32),
            pltpu.VMEM((nb, CORES * MOST, QB), F32),
            dma((4,)),
            dma((zn, CORES)),
            dma((zn, CORES)),
            dma((zn, XN)),
            dma((zn, XN)),
            dma((2,)),
            dma((2,)),
            dma((yn, CORES)),
            dma((yn, CORES)),
            dma((XN, nb)),
            dma((XN, nb)),
            dma((nb,)),
            dma((zn,)),
            dma((zn,)),
            dma((zn,)),
            dma((zn, XN)),
            dma((zn, XN)),
            dma,
            dma,
            pltpu.SemaphoreType.REGULAR,
        ],
        compiler_params=pltpu.CompilerParams(
            collective_id=0, has_side_effects=True, vmem_limit_bytes=64 * 2**20
        ),
        cost_estimate=pl.CostEstimate(flops=3 * 10**9, bytes_accessed=4 * 10**6, transcendentals=3 * 10**6),
    )(queries, keys, values, pattern, out_weight.T).T


def solution(mesh):
    in_specs = (P("rows", "heads"), P("rows", "heads"), P("rows", "heads"), P(), P("heads", "rows"))
    out_specs = P("heads", "rows")
    return jax.shard_map(shards, mesh=mesh, in_specs=in_specs, out_specs=out_specs, check_vma=False)
```

time: 363 us -> 75.2 us (0.21); the launches traced: 358 us -> 75 us
  waiting for transfers between devices: 266 us -> 0 us
  Pallas kernels: 0 us -> 73.7 us
  local copies, waits for them, and re-layouts: 28.3 us -> 1.35 us
  blocking collectives: 19.5 us -> 0 us
  matrix products: 15.4 us -> 0 us
  between operations: 13.2 us -> 0.01 us
  other arithmetic: 10.5 us -> 0 us
  starting transfers between devices: 5.31 us -> 0 us
    all_gather x2 -> x0, waiting for transfers between devices: 167 us -> none  [the longest x1 87 us: shards(): every_query = lax.all_gather(queries, 'rows', axis=0, tiled=True)]
    pallas_call x0 -> x1, Pallas kernels: none -> 73.7 us  [shards(): pl.pallas_call(kernel, name='attend_project', out_shape=jax.ShapeDtypeStr...]
    all_to_all x1 -> x0, waiting for transfers between devices: 66.2 us -> none  [spread_merge(): lax.all_to_all(send_out, 'rows', split_axis=0, concat_axis=0, tiled=True)]
    reduce_scatter x1 -> x0, waiting for transfers between devices: 31.4 us -> none  [shards(): lax.psum_scatter(projected, 'heads', scatter_dimension=0, tiled=True)]
    all_to_all x1 -> x0, blocking collectives: 19.5 us -> none  [spread_merge(): lax.all_to_all(send_lse, 'rows', split_axis=0, concat_axis=0, tiled=True)]
    dot_general x17 -> x0, matrix products: 15.4 us -> none  [the longest x8 7.07 us: block_partial(): jnp.einsum('hqk,khd->qhd', weights, value_heads, preferred_element_type=j...]
    dynamic_slice x16 -> x0, local copies, waits for them, and re-layouts: 8.83 us -> none  [spread_merge(): lax.map(lambda query_block: block_partial(query_block, key_heads, value_h...]
    reduce_sum x10 -> x0, other arithmetic: 8.12 us -> none  [the longest x8 5.72 us: block_partial(): row_total = jnp.sum(exp_scores, axis=2)]
  transfers between devices with their start and end apart: 4 -> 0, of which waited for: 4 -> 0; matrix products, arithmetic and copies ran while one was open for 3% -> 0% of each run, Pallas kernels for 0% -> 0%
where the time goes in v1:
time: 75.2 us; the launch traced here: 75 us
  Pallas kernels  73.7 us (98%)
  local copies, waits for them, and re-layouts  1.35 us (2%)
    pallas_call x1, Pallas kernels, shards(): pl.pallas_call(kernel, name='attend_project', out_shape=jax.ShapeDtypeStr...  73.7 us

profile of v1, /device:TPU:1, one launch (start us, length us, event | category | flops | bytes accessed | tf_op | source)
XLA Modules:
  0.0 75.0 jit_solution(6820437368878795695)
XLA Ops:
  0.0 73.7 %attend_project.1 = bf16[96,128]{1,0:T(8,128)(2,1)} custom-call(bf16[16,768]{1,0:T(8,128)(2,1)} %q_ref.1, bf16[1024,768]{1,0:T(8,128)(2,1)} %k_ref.1, bf16[1024,768]{1,0:T(8,128)(2,1)} %v_ref.1, s32[8,16]{1,0:T(8,128)} %pat_ref.1, bf16[96,768]{1,0:T(8,128)(2,1)} %bitcast.3), custom_call_target="tpu_custom_call" | custom-call | flops 3000000000 | bytes 4000000 | tf_op jit(solution)/shard_map/attend_project/pallas_call | solution.py:404
  73.7 1.3 %copy.7 = bf16[128,96]{0,1:T(8,128)(2,1)} copy(bf16[128,96]{0,1:T(8,128)(2,1)} %bitcast.2) | data formatting | bytes 49152

commit v2 on v1

v2 whole, which is shorter than its diff:
```python
import functools
import math

import jax
import jax.numpy as jnp
from jax import lax
from jax.experimental import pallas as pl
from jax.experimental.pallas import tpu as pltpu
from jax.sharding import PartitionSpec as P

MESH = pl.DeviceIdType.MESH
HD = 128
QB = 128
MOST = 4
CORES = 2
XN = 4
STATS = 16
LANES = 128
LOW = -(2.0**100)
NT = (((1,), (1,)), ((), ()))
BF = jnp.bfloat16
F32 = jnp.float32


def near_first(n):
    order = []
    for step in range(1, n // 2 + 1):
        order.append(step)
        if n - step != step:
            order.append(n - step)
    return order


def kernel(
    q_ref,
    k_ref,
    v_ref,
    pat_ref,
    w_ref,
    out_ref,
    q_all,
    k_buf,
    v_buf,
    v_t,
    w_in,
    w_piece,
    w_mine,
    w_wide,
    w_all,
    w_turned,
    q_sel,
    score,
    peak,
    num,
    top,
    tot,
    parts,
    parts_in,
    ends,
    ends_in,
    weight,
    stat_m,
    stat_l,
    sums,
    sums_in,
    att,
    out_part,
    out_in,
    masks,
    local_sem,
    qz_s,
    qz_r,
    qx_s,
    qx_r,
    kv_s,
    kv_r,
    wx_s,
    wx_r,
    wy_s,
    wy_r,
    qh_s,
    qh_r,
    rx_s,
    rx_r,
    rz_s,
    rz_r,
    az_s,
    az_r,
    out_s,
    out_r,
    ready,
):
    r = lax.axis_index("rows")
    y = lax.axis_index("heads")
    yn = w_all.shape[0]
    zn = att.shape[0]
    nb = zn
    heads = num.shape[2] // HD
    half = heads * HD
    dq = HD // XN
    body = heads * dq
    own = q_ref.shape[0]
    z = r // (XN * CORES)
    x = (r // CORES) % XN
    c = r % CORES
    sib = 1 - c

    def dev(dz, dx, dc, dy):
        return ((dz * XN + dx) * CORES + dc, dy)

    def remote(src, dst, ss, rs, to):
        return pltpu.make_async_remote_copy(
            src_ref=src, dst_ref=dst, send_sem=ss, recv_sem=rs, device_id=to, device_id_type=MESH
        )

    def mod(v, n):
        return lax.rem(v + n, n)

    def half_of(which):
        return pl.ds(pl.multiple_of(which * half, HD), half)

    def q_rows(zz, xx, cc):
        return pl.ds(pl.multiple_of((zz * XN + xx) * (CORES * own) + cc * own, own), own)

    def q_pair(zz, xx):
        return pl.ds(pl.multiple_of((zz * XN + xx) * (CORES * own), CORES * own), CORES * own)

    k_own = pltpu.make_async_copy(k_ref.at[:, half_of(c)], k_buf.at[c], local_sem.at[0])
    v_own = pltpu.make_async_copy(v_ref.at[:, half_of(c)], v_buf.at[c], local_sem.at[1])
    q_own = pltpu.make_async_copy(q_ref.at[:, half_of(c)], q_all.at[q_rows(z, x, c)], local_sem.at[2])
    w_own = pltpu.make_async_copy(w_ref, w_in.at[0 : w_ref.shape[0]], local_sem.at[3])
    q_own.start()
    w_own.start()
    v_own.start()
    k_own.start()

    bar = pltpu.get_barrier_semaphore()

    def signal(to):
        pl.semaphore_signal(bar, inc=1, device_id=to, device_id_type=MESH)

    near = (1, -1, 2, -2)
    far = ((2, (-1, -2)), (-2, (1,)))
    onward = {2: (1, 2), -2: (-1,)}
    group = [(e, f) for e in (2, 1, 3, 0) for f in (1, 0) if e or f]
    for d in reversed(near_first(zn)):
        signal(dev(mod(z + d, zn), x, c, y))
    for d in reversed(near_first(yn)):
        signal(dev(z, x, c, mod(y + d, yn)))
    for e, f in group:
        signal(dev(z, mod(x + e, XN), mod(c + f, CORES), y))
    signals = zn - 1 + yn - 1 + len(group)

    pl.semaphore_wait(bar, signals)

    q_sib = remote(q_ref.at[:, half_of(sib)], q_all.at[q_rows(z, x, c)], qz_s.at[0], qz_r.at[0], dev(z, x, sib, y))
    q_sib.start()

    def arrived(dst, sem):
        pltpu.make_async_copy(dst, dst, sem).wait()

    q_own.wait()
    arrived(q_all.at[q_rows(z, x, sib)], qz_r.at[0])

    def along_z(ref, origin, hop, distance, ss, rs):
        copy = remote(ref, ref, ss.at[distance % zn], rs.at[distance % zn], dev(mod(z + hop, zn), x, c, y))
        copy.start()
        return copy

    def pair_from(d):
        return q_all.at[q_pair(mod(z - d, zn), x)]

    qz, qx = [], []

    def along_x(d):
        for e in near_first(XN):
            pair = pair_from(d)
            copy = remote(pair, pair, qx_s.at[d % zn, e], qx_r.at[d % zn, e], dev(z, mod(x + e, XN), c, y))
            copy.start()
            qx.append(copy)

    for d in near:
        qz.append(along_z(pair_from(0), 0, d, d, qz_s, qz_r))
    along_x(0)
    kv = [
        remote(ref.at[:, half_of(sib)], buf.at[c], kv_s.at[i], kv_r.at[i], dev(z, x, sib, y))
        for i, (ref, buf) in enumerate(((k_ref, k_buf), (v_ref, v_buf)))
    ]
    for copy in kv:
        copy.start()
    for d in range(1, yn):
        pl.semaphore_signal(ready, inc=1, device_id=dev(z, x, c, mod(y + d, yn)), device_id_type=MESH)

    w_in[w_ref.shape[0] :, :] = jnp.zeros((LANES - w_ref.shape[0], w_in.shape[1]), BF)
    w_own.wait()
    for cc in range(CORES):
        for h in range(heads):
            first = cc * half + h * HD
            turned = w_in[:, first : first + HD].astype(F32).T.astype(BF)
            for xx in range(XN):
                w_piece[xx, cc, h * dq : (h + 1) * dq, :] = turned[xx * dq : (xx + 1) * dq]
    w_mine[x, c] = w_piece[x, c]
    wx = []
    for e, f in group:
        to = mod(x + e, XN), mod(c + f, CORES)
        copy = remote(w_piece.at[to[0], to[1]], w_mine.at[x, c], wx_s.at[e, f], wx_r.at[e, f], dev(z, to[0], to[1], y))
        copy.start()
        wx.append(copy)

    top[...] = jnp.zeros_like(top)
    tot[...] = jnp.zeros_like(tot)
    stat_m[...] = jnp.zeros_like(stat_m)
    stat_l[...] = jnp.zeros_like(stat_l)

    for cb in range(CORES):
        hit = (pat_ref[...] == (z * XN + x) * CORES + cb).astype(F32)
        linked = jnp.max(hit, axis=1, keepdims=True)
        count = jnp.zeros((1, QB), F32)
        for b in range(nb):
            this = jnp.broadcast_to(linked[b : b + 1], (1, QB))
            for j in range(MOST):
                masks[b, cb * MOST + j : cb * MOST + j + 1, :] = jnp.where(count == j, this, 0.0)
            count = count + this
    for d in (2, -2, 1, -1):
        arrived(pair_from(d), qz_r.at[d % zn])
        for hop in onward.get(d, ()):
            qz.append(along_z(pair_from(d), d, hop, d + hop, qz_s, qz_r))
        along_x(d)

    for e, f in group:
        arrived(w_mine.at[mod(x - e, XN), mod(c - f, CORES)], wx_r.at[e, f])
    cols = out_ref.shape[0]
    every = [w_mine[xx, cc][:, 0:cols] for xx in range(XN) for cc in range(CORES)]
    w_wide[...] = jnp.concatenate(every, axis=1)
    wy = []

    def weights(src, origin, to, which):
        copy = remote(src, w_all.at[mod(origin + to + yn, yn)], wy_s.at[which], wy_r.at[which], dev(z, x, c, mod(to + yn, yn)))
        copy.start()
        wy.append(copy)

    for d in near:
        weights(w_wide, y, y + d, d % yn)
    w_all[mod(y + y, yn)] = w_wide[...]
    distant = (3, -3, 4)
    for d in distant:
        arrived(pair_from(d), qz_r.at[d % zn])

    def head_of(d, xx, h):
        return q_all.at[q_pair(mod(z - d, zn), xx), pl.ds(h * HD, HD)]

    for h in range(heads):
        for n, d in enumerate(distant):
            for e in near_first(XN):
                mine = head_of(d, x, h)
                copy = remote(mine, mine, qh_s.at[h, n, e], qh_r.at[h, n, e], dev(z, mod(x + e, XN), c, y))
                copy.start()
                qx.append(copy)
    v_own.wait()
    for h in range(heads):
        v_t[c, h * HD : (h + 1) * HD, :] = v_buf[c, :, h * HD : (h + 1) * HD].T
    k_own.wait()
    for copy in kv:
        copy.wait_recv()
    for h in range(heads):
        v_t[sib, h * HD : (h + 1) * HD, :] = v_buf[sib, :, h * HD : (h + 1) * HD].T
    for d in (0,) + near:
        for e in near_first(XN):
            arrived(q_all.at[q_pair(mod(z - d, zn), mod(x - e, XN))], qx_r.at[d % zn, e])

    scale = HD**-0.5 * math.log2(math.e)

    def choose(h):
        for n, d in enumerate(distant):
            for e in near_first(XN):
                arrived(head_of(d, mod(x - e, XN), h), qh_r.at[h, n, e])
        cols = slice(h * HD, (h + 1) * HD)

        def slot(i, _):
            rows = pl.ds(pl.multiple_of((i % MOST) * QB, QB), QB)
            picked = [masks[b, pl.ds(i, 1), :].astype(BF) * q_all[b * QB : (b + 1) * QB, cols] for b in range(nb)]
            q_sel[i // MOST, h, rows, :] = functools.reduce(jnp.add, picked)
            return 0

        lax.fori_loop(0, CORES * MOST, slot, 0)

    def front(h, cb):
        cols = slice(h * HD, (h + 1) * HD)
        s = lax.dot_general(k_buf[cb, :, cols], q_sel[cb, h], NT, preferred_element_type=F32)
        score[cb] = s
        peak[cb] = jnp.broadcast_to(jnp.max(s, axis=0, keepdims=True) * scale, (8, MOST * QB))

    def back(h, cb):
        cols = slice(h * HD, (h + 1) * HD)
        m = peak[cb, 0:1]
        e = jnp.exp2(score[cb] * scale - m)
        l = jnp.sum(e, axis=0, keepdims=True)
        o = jnp.dot(v_t[cb, cols, :], e.astype(BF), preferred_element_type=F32)
        for j in range(MOST):
            lanes = slice(j * QB, (j + 1) * QB)
            num[cb, j, cols, :] = o[:, lanes]
            top[cb, j, h : h + 1, :] = m[:, lanes]
            tot[cb, j, h : h + 1, :] = l[:, lanes]

    row = lax.broadcasted_iota(jnp.int32, (8, QB), 0)

    def stats_of(m, l):
        high = l.astype(BF).astype(F32)
        first = jnp.where(row < heads, m, pltpu.roll(high, heads, 0))
        return jnp.concatenate([first, l - high], axis=0).astype(BF)

    def read_stats(block):
        block = block.astype(F32)
        first = block[0:8]
        return first, pltpu.roll(first, 8 - heads, 0) + block[8:16]

    rx = []
    slots = range(CORES * MOST)

    def turn(i):
        return mod(z - y + i + 1 + yn, nb)

    def partial(h, b, xx):
        f = weight[b, h]
        rows = slice(h * HD + xx * dq, h * HD + (xx + 1) * dq)
        terms = [f[i : i + 1] * num[i // MOST, i % MOST, rows, :] for i in slots]
        return functools.reduce(jnp.add, terms).astype(BF)

    def weigh(h, b):
        mask = masks[b]
        tops = jnp.concatenate([top[i // MOST, i % MOST, h : h + 1, :] for i in slots], axis=0)
        tots = jnp.concatenate([tot[i // MOST, i % MOST, h : h + 1, :] for i in slots], axis=0)
        tops = jnp.where(mask > 0.5, tops, LOW)
        m = jnp.max(tops, axis=0, keepdims=True).astype(BF).astype(F32)
        f = jnp.exp2(tops - m)
        weight[b, h] = f
        stat_m[b, h : h + 1, :] = m
        stat_l[b, h : h + 1, :] = jnp.sum(f * tots, axis=0, keepdims=True)

    choose(0)
    front(0, 0)
    for h in range(heads):
        front(h, 1)
        back(h, 0)
        if h + 1 < heads:
            choose(h + 1)
            front(h + 1, 0)
        back(h, 1)
        if h + 1 < heads:

            def whole(b, _):
                weigh(h, b)
                for xx in range(XN):
                    parts[xx, h, b] = partial(h, b, xx)
                return 0

            lax.fori_loop(0, nb, whole, 0)
            for e in near_first(XN):
                to = mod(x + e, XN)
                copy = remote(parts.at[to, h], parts_in.at[e, h], rx_s.at[e, nb + h], rx_r.at[e, nb + h], dev(z, to, c, y))
                copy.start()
                rx.append(copy)
        if h == 0:
            for d, hops in far:
                origin = y + d
                arrived(w_all.at[mod(y + origin + yn, yn)], wy_r.at[-d % yn])
                for hop in hops:
                    weights(w_all.at[mod(origin + y + yn, yn)], origin, y + hop, (hop - d) % yn)

    for i in range(nb):
        b = turn(i)
        weigh(heads - 1, b)
        stats = stats_of(stat_m[b], stat_l[b])
        for xx in range(XN):
            ends[xx, b, 0:dq, :] = partial(heads - 1, b, xx)
            ends[xx, b, dq:, :] = stats
        for e in near_first(XN):
            to = mod(x + e, XN)
            copy = remote(ends.at[to, b], ends_in.at[e, b], rx_s.at[e, i], rx_r.at[e, i], dev(z, to, c, y))
            copy.start()
            rx.append(copy)

    def merge(all_stats, blocks):
        stats = [read_stats(block) for block in all_stats]
        m = functools.reduce(jnp.maximum, [s[0] for s in stats])
        factors = [jnp.exp2(s[0] - m) for s in stats]
        l = functools.reduce(jnp.add, [f * s[1] for f, s in zip(factors, stats)])
        sums_of = []
        for h in range(heads):
            terms = [f[h : h + 1] * block.astype(F32) for f, block in zip(factors, blocks[h])]
            sums_of.append(functools.reduce(jnp.add, terms))
        return sums_of, m, l

    pl.semaphore_wait(ready, yn - 1)
    for h in range(heads - 1):
        for e in near_first(XN):
            arrived(parts_in.at[e, h], rx_r.at[e, nb + h])
    for i in range(nb):
        b = turn(i)
        for e in near_first(XN):
            arrived(ends_in.at[e, b], rx_r.at[e, i])
        blocks = [[parts[x, h, b]] + [parts_in[e, h, b] for e in near_first(XN)] for h in range(heads - 1)]
        got = [ends[x, b]] + [ends_in[e, b] for e in near_first(XN)]
        blocks.append([block[0:dq] for block in got])
        merged, m, l = merge([block[dq:] for block in got], blocks)
        for h in range(heads):
            sums[i, h * dq : (h + 1) * dq, :] = merged[h].astype(BF)
        sums[i, body:, :] = stats_of(m, l)
        zz = mod(z + i + 1, zn)
        here = jnp.logical_and(zz == z, b == y)

        @pl.when(here)
        def _():
            pltpu.make_async_copy(sums.at[i], sums_in.at[z], rz_r.at[z]).start()

        @pl.when(jnp.logical_not(here))
        def _():
            remote(sums.at[i], sums_in.at[z], rz_s.at[i], rz_r.at[z], dev(zz, x, c, b)).start()

    for zz in range(zn):
        arrived(sums_in.at[zz], rz_r.at[zz])
    got = [sums_in[zz] for zz in range(zn)]
    blocks = [[block[h * dq : (h + 1) * dq] for block in got] for h in range(heads)]
    merged, m, l = merge([block[body:] for block in got], blocks)
    for h in range(heads):
        att[z, h * dq : (h + 1) * dq, :] = (merged[h] / l[h : h + 1]).astype(BF)

    def rz_wait():
        for i in range(nb):
            b = turn(i)
            here = jnp.logical_and(mod(z + i + 1, zn) == z, b == y)

            @pl.when(jnp.logical_not(here))
            def _():
                remote(sums.at[i], sums_in.at[z], rz_s.at[i], rz_r.at[z], dev(z, x, c, y)).wait_send()

    az = [along_z(att.at[z], 0, d, d, az_s, az_r) for d in near]
    for d in (2, -2):
        piece = att.at[mod(z - d, zn)]
        arrived(piece, az_r.at[d % zn])
        for hop in onward[d]:
            az.append(along_z(piece, d, hop, d + hop, az_s, az_r))
    for d in range(1, yn):
        if d not in (2, yn - 2):
            arrived(w_all.at[mod(y + y - d + yn, yn)], wy_r.at[d])
    w_turned[...] = w_all[...].reshape(zn * body, w_all.shape[2]).T
    for d in (1, -1, 3, -3, 4):
        arrived(att.at[mod(z - d, zn)], az_r.at[d % zn])

    rows = att[...].reshape(zn * body, QB)
    outs = []
    for e, f in group + [(0, 0)]:
        xx, cc = mod(x + e, XN), mod(c + f, CORES)
        wide = w_turned[pl.ds(pl.multiple_of((xx * CORES + cc) * cols, cols), cols), :]
        term = jnp.dot(wide, rows, preferred_element_type=F32)
        if e or f:
            out_part[xx, cc] = term.astype(BF)
            copy = remote(out_part.at[xx, cc], out_in.at[e, f], out_s.at[e, f], out_r.at[e, f], dev(z, xx, cc, y))
            copy.start()
            outs.append(copy)
    for sent in ([q_sib], qz, qx, kv, wx, wy, rx, az):
        for copy in sent:
            copy.wait_send()
    rz_wait()
    for copy in outs:
        copy.wait()
    for e, f in group:
        term = term + out_in[e, f].astype(F32)
    out_ref[...] = term.astype(BF)


def shards(queries, keys, values, pattern, out_weight):
    yn = lax.axis_size("heads")
    zn = lax.axis_size("rows") // (XN * CORES)
    nb = pattern.shape[0]
    own, width = queries.shape
    half = width // CORES
    heads = half // HD
    cblk = keys.shape[0]
    cols = out_weight.shape[1]
    piece = heads * (HD // XN)
    load = piece + STATS
    dma = pltpu.SemaphoreType.DMA
    anywhere = pl.BlockSpec(memory_space=pl.ANY)
    return pl.pallas_call(
        kernel,
        name="attend_project",
        out_shape=jax.ShapeDtypeStruct((cols, QB), BF),
        in_specs=[anywhere, anywhere, anywhere, pl.BlockSpec(memory_space=pltpu.VMEM), anywhere],
        out_specs=pl.BlockSpec(memory_space=pltpu.VMEM),
        scratch_shapes=[
            pltpu.VMEM((nb * QB, half), BF),
            pltpu.VMEM((CORES, cblk, half), BF),
            pltpu.VMEM((CORES, cblk, half), BF),
            pltpu.VMEM((CORES, half, cblk), BF),
            pltpu.VMEM((LANES, width), BF),
            pltpu.VMEM((XN, CORES, piece, LANES), BF),
            pltpu.VMEM((XN, CORES, piece, LANES), BF),
            pltpu.VMEM((piece, XN * CORES * cols), BF),
            pltpu.VMEM((yn, piece, XN * CORES * cols), BF),
            pltpu.VMEM((XN * CORES * cols, zn * piece), BF),
            pltpu.VMEM((CORES, heads, MOST * QB, HD), BF),
            pltpu.VMEM((2, cblk, MOST * QB), F32),
            pltpu.VMEM((2, 8, MOST * QB), F32),
            pltpu.VMEM((CORES, MOST, half, QB), F32),
            pltpu.VMEM((CORES, MOST, 8, QB), F32),
            pltpu.VMEM((CORES, MOST, 8, QB), F32),
            pltpu.VMEM((XN, heads - 1, nb, HD // XN, QB), BF),
            pltpu.VMEM((XN, heads - 1, nb, HD // XN, QB), BF),
            pltpu.VMEM((XN, nb, HD // XN + STATS, QB), BF),
            pltpu.VMEM((XN, nb, HD // XN + STATS, QB), BF),
            pltpu.VMEM((nb, heads, CORES * MOST, QB), F32),
            pltpu.VMEM((nb, 8, QB), F32),
            pltpu.VMEM((nb, 8, QB), F32),
            pltpu.VMEM((nb, load, QB), BF),
            pltpu.VMEM((zn, load, QB), BF),
            pltpu.VMEM((zn, piece, QB), BF),
            pltpu.VMEM((XN, CORES, cols, QB), BF),
            pltpu.VMEM((XN, CORES, cols, QB), BF),
            pltpu.VMEM((nb, CORES * MOST, QB), F32),
            dma((4,)),
            dma((zn,)),
            dma((zn,)),
            dma((zn, XN)),
            dma((zn, XN)),
            dma((2,)),
            dma((2,)),
            dma((XN, CORES)),
            dma((XN, CORES)),
            dma((yn,)),
            dma((yn,)),
            dma((heads, 3, XN)),
            dma((heads, 3, XN)),
            dma((XN, nb + heads - 1)),
            dma((XN, nb + heads - 1)),
            dma((nb,)),
            dma((zn,)),
            dma((zn,)),
            dma((zn,)),
            dma((XN, CORES)),
            dma((XN, CORES)),
            pltpu.SemaphoreType.REGULAR,
        ],
        compiler_params=pltpu.CompilerParams(
            collective_id=0, has_side_effects=True, vmem_limit_bytes=64 * 2**20
        ),
        cost_estimate=pl.CostEstimate(flops=3 * 10**9, bytes_accessed=4 * 10**6, transcendentals=3 * 10**6),
    )(queries, keys, values, pattern, out_weight.T).T


def solution(mesh):
    in_specs = (P("rows", "heads"), P("rows", "heads"), P("rows", "heads"), P(), P("heads", "rows"))
    out_specs = P("heads", "rows")
    return jax.shard_map(shards, mesh=mesh, in_specs=in_specs, out_specs=out_specs, check_vma=False)
```

time: 75.2 us -> 70.5 us (0.938)
  Pallas kernels: 73.7 us -> 69 us
    pallas_call x1, Pallas kernels: 73.7 us -> 69 us  [shards(): pl.pallas_call(kernel, name='attend_project', out_shape=jax.ShapeDtypeStr...]
where the time goes in v2:
time: 70.5 us; the launch traced here: 70.3 us
  Pallas kernels  69 us (98%)
  local copies, waits for them, and re-layouts  1.35 us (2%)
    pallas_call x1, Pallas kernels, shards(): pl.pallas_call(kernel, name='attend_project', out_shape=jax.ShapeDtypeStr...  69 us

profile of v2, /device:TPU:1, one launch (start us, length us, event | category | flops | bytes accessed | tf_op | source)
XLA Modules:
  0.0 70.3 jit_solution(5745564809497865437)
XLA Ops:
  0.0 69.0 %attend_project.1 = bf16[96,128]{1,0:T(8,128)(2,1)} custom-call(bf16[16,768]{1,0:T(8,128)(2,1)} %q_ref.1, bf16[1024,768]{1,0:T(8,128)(2,1)} %k_ref.1, bf16[1024,768]{1,0:T(8,128)(2,1)} %v_ref.1, s32[8,16]{1,0:T(8,128)} %pat_ref.1, bf16[96,768]{1,0:T(8,128)(2,1)} %bitcast.3), custom_call_target="tpu_custom_call" | custom-call | flops 3000000000 | bytes 4000000 | tf_op jit(solution)/shard_map/attend_project/pallas_call | solution.py:485
  69.0 1.3 %copy.7 = bf16[128,96]{0,1:T(8,128)(2,1)} copy(bf16[128,96]{0,1:T(8,128)(2,1)} %bitcast.2) | data formatting | bytes 49152

commit v3 on v2

--- a/solution.py
+++ b/solution.py
@@ -89,6 +89,7 @@
     out_s,
     out_r,
     ready,
+    ready_all,
 ):
     r = lax.axis_index("rows")
     y = lax.axis_index("heads")
@@ -143,34 +144,40 @@
     far = ((2, (-1, -2)), (-2, (1,)))
     onward = {2: (1, 2), -2: (-1,)}
     group = [(e, f) for e in (2, 1, 3, 0) for f in (1, 0) if e or f]
-    for d in reversed(near_first(zn)):
-        signal(dev(mod(z + d, zn), x, c, y))
-    for d in reversed(near_first(yn)):
+    for d in reversed(near):
+        for cc in range(CORES):
+            signal(dev(mod(z + d, zn), x, cc, y))
         signal(dev(z, x, c, mod(y + d, yn)))
     for e, f in group:
         signal(dev(z, mod(x + e, XN), mod(c + f, CORES), y))
-    signals = zn - 1 + yn - 1 + len(group)
+    signals = len(near) * (CORES + 1) + len(group)
 
     pl.semaphore_wait(bar, signals)
 
-    q_sib = remote(q_ref.at[:, half_of(sib)], q_all.at[q_rows(z, x, c)], qz_s.at[0], qz_r.at[0], dev(z, x, sib, y))
-    q_sib.start()
+    rows_here = q_all.at[q_rows(z, x, c)]
+    qz, qx = [], []
+
+    def half_to(cc, d, ss):
+        copy = remote(q_ref.at[:, half_of(cc)], rows_here, ss, qz_r.at[d % zn, c], dev(mod(z + d, zn), x, cc, y))
+        copy.start()
+        qz.append(copy)
+
+    half_to(sib, 0, qz_s.at[0, 0])
+    for d in near:
+        for cc in range(CORES):
+            half_to(cc, d, qz_s.at[d % zn, cc])
 
     def arrived(dst, sem):
         pltpu.make_async_copy(dst, dst, sem).wait()
 
-    q_own.wait()
-    arrived(q_all.at[q_rows(z, x, sib)], qz_r.at[0])
-
     def along_z(ref, origin, hop, distance, ss, rs):
-        copy = remote(ref, ref, ss.at[distance % zn], rs.at[distance % zn], dev(mod(z + hop, zn), x, c, y))
+        copy = remote(ref, ref, ss(distance % zn), rs(distance % zn), dev(mod(z + hop, zn), x, c, y))
         copy.start()
         return copy
 
     def pair_from(d):
         return q_all.at[q_pair(mod(z - d, zn), x)]
 
-    qz, qx = [], []
 
     def along_x(d):
         for e in near_first(XN):
@@ -179,8 +186,8 @@
             copy.start()
             qx.append(copy)
 
-    for d in near:
-        qz.append(along_z(pair_from(0), 0, d, d, qz_s, qz_r))
+    q_own.wait()
+    arrived(q_all.at[q_rows(z, x, sib)], qz_r.at[0, sib])
     along_x(0)
     kv = [
         remote(ref.at[:, half_of(sib)], buf.at[c], kv_s.at[i], kv_r.at[i], dev(z, x, sib, y))
@@ -188,8 +195,6 @@
     ]
     for copy in kv:
         copy.start()
-    for d in range(1, yn):
-        pl.semaphore_signal(ready, inc=1, device_id=dev(z, x, c, mod(y + d, yn)), device_id_type=MESH)
 
     w_in[w_ref.shape[0] :, :] = jnp.zeros((LANES - w_ref.shape[0], w_in.shape[1]), BF)
     w_own.wait()
@@ -222,9 +227,10 @@
                 masks[b, cb * MOST + j : cb * MOST + j + 1, :] = jnp.where(count == j, this, 0.0)
             count = count + this
     for d in (2, -2, 1, -1):
-        arrived(pair_from(d), qz_r.at[d % zn])
+        for cc in range(CORES):
+            arrived(q_all.at[q_rows(mod(z - d, zn), x, cc)], qz_r.at[d % zn, cc])
         for hop in onward.get(d, ()):
-            qz.append(along_z(pair_from(d), d, hop, d + hop, qz_s, qz_r))
+            qz.append(along_z(pair_from(d), d, hop, d + hop, lambda n: qz_s.at[n, 0], lambda n: qz_r.at[n, 0]))
         along_x(d)
 
     for e, f in group:
@@ -239,12 +245,18 @@
         copy.start()
         wy.append(copy)
 
-    for d in near:
+    for d in (2, -2, 1, -1):
         weights(w_wide, y, y + d, d % yn)
     w_all[mod(y + y, yn)] = w_wide[...]
     distant = (3, -3, 4)
     for d in distant:
-        arrived(pair_from(d), qz_r.at[d % zn])
+        arrived(pair_from(d), qz_r.at[d % zn, 0])
+
+    def tell(sem):
+        for d in near:
+            pl.semaphore_signal(sem, inc=1, device_id=dev(z, x, c, mod(y + d, yn)), device_id_type=MESH)
+
+    tell(ready)
 
     def head_of(d, xx, h):
         return q_all.at[q_pair(mod(z - d, zn), xx), pl.ds(h * HD, HD)]
@@ -361,6 +373,9 @@
                 copy.start()
                 rx.append(copy)
         if h == 0:
+            pl.semaphore_wait(ready, len(near))
+            tell(ready_all)
+        if h == 1:
             for d, hops in far:
                 origin = y + d
                 arrived(w_all.at[mod(y + origin + yn, yn)], wy_r.at[-d % yn])
@@ -391,7 +406,7 @@
             sums_of.append(functools.reduce(jnp.add, terms))
         return sums_of, m, l
 
-    pl.semaphore_wait(ready, yn - 1)
+    pl.semaphore_wait(ready_all, len(near))
     for h in range(heads - 1):
         for e in near_first(XN):
             arrived(parts_in.at[e, h], rx_r.at[e, nb + h])
@@ -434,12 +449,12 @@
             def _():
                 remote(sums.at[i], sums_in.at[z], rz_s.at[i], rz_r.at[z], dev(z, x, c, y)).wait_send()
 
-    az = [along_z(att.at[z], 0, d, d, az_s, az_r) for d in near]
+    az = [along_z(att.at[z], 0, d, d, lambda n: az_s.at[n], lambda n: az_r.at[n]) for d in near]
     for d in (2, -2):
         piece = att.at[mod(z - d, zn)]
         arrived(piece, az_r.at[d % zn])
         for hop in onward[d]:
-            az.append(along_z(piece, d, hop, d + hop, az_s, az_r))
+            az.append(along_z(piece, d, hop, d + hop, lambda n: az_s.at[n], lambda n: az_r.at[n]))
     for d in range(1, yn):
         if d not in (2, yn - 2):
             arrived(w_all.at[mod(y + y - d + yn, yn)], wy_r.at[d])
@@ -458,7 +473,7 @@
             copy = remote(out_part.at[xx, cc], out_in.at[e, f], out_s.at[e, f], out_r.at[e, f], dev(z, xx, cc, y))
             copy.start()
             outs.append(copy)
-    for sent in ([q_sib], qz, qx, kv, wx, wy, rx, az):
+    for sent in (qz, qx, kv, wx, wy, rx, az):
         for copy in sent:
             copy.wait_send()
     rz_wait()
@@ -519,8 +534,8 @@
             pltpu.VMEM((XN, CORES, cols, QB), BF),
             pltpu.VMEM((nb, CORES * MOST, QB), F32),
             dma((4,)),
-            dma((zn,)),
-            dma((zn,)),
+            dma((zn, CORES)),
+            dma((zn, CORES)),
             dma((zn, XN)),
             dma((zn, XN)),
             dma((2,)),
@@ -540,6 +555,7 @@
             dma((XN, CORES)),
             dma((XN, CORES)),
             pltpu.SemaphoreType.REGULAR,
+            pltpu.SemaphoreType.REGULAR,
         ],
         compiler_params=pltpu.CompilerParams(
             collective_id=0, has_side_effects=True, vmem_limit_bytes=64 * 2**20

time: 70.5 us -> 67.7 us (0.960)
  Pallas kernels: 69 us -> 66 us
    pallas_call x1, Pallas kernels: 69 us -> 66 us  [shards(): pl.pallas_call(kernel, name='attend_project', out_shape=jax.ShapeDtypeStr...]
where the time goes in v3:
time: 67.7 us; the launch traced here: 67.4 us
  Pallas kernels  66 us (97%)
  local copies, waits for them, and re-layouts  1.35 us (2%)
    pallas_call x1, Pallas kernels, shards(): pl.pallas_call(kernel, name='attend_project', out_shape=jax.ShapeDtypeStr...  66 us

profile of v3, /device:TPU:1, one launch (start us, length us, event | category | flops | bytes accessed | tf_op | source)
XLA Modules:
  0.0 67.4 jit_solution(12552550411138102849)
XLA Ops:
  0.0 66.0 %attend_project.1 = bf16[96,128]{1,0:T(8,128)(2,1)} custom-call(bf16[16,768]{1,0:T(8,128)(2,1)} %q_ref.1, bf16[1024,768]{1,0:T(8,128)(2,1)} %k_ref.1, bf16[1024,768]{1,0:T(8,128)(2,1)} %v_ref.1, s32[8,16]{1,0:T(8,128)} %pat_ref.1, bf16[96,768]{1,0:T(8,128)(2,1)} %bitcast.3), custom_call_target="tpu_custom_call" | custom-call | flops 3000000000 | bytes 4000000 | tf_op jit(solution)/shard_map/attend_project/pallas_call | solution.py:500
  66.0 1.3 %copy.7 = bf16[128,96]{0,1:T(8,128)(2,1)} copy(bf16[128,96]{0,1:T(8,128)(2,1)} %bitcast.2) | data formatting | bytes 49152

commit v4 on v3

--- a/solution.py
+++ b/solution.py
@@ -375,13 +375,6 @@
         if h == 0:
             pl.semaphore_wait(ready, len(near))
             tell(ready_all)
-        if h == 1:
-            for d, hops in far:
-                origin = y + d
-                arrived(w_all.at[mod(y + origin + yn, yn)], wy_r.at[-d % yn])
-                for hop in hops:
-                    weights(w_all.at[mod(origin + y + yn, yn)], origin, y + hop, (hop - d) % yn)
-
     for i in range(nb):
         b = turn(i)
         weigh(heads - 1, b)
@@ -394,6 +387,12 @@
             copy = remote(ends.at[to, b], ends_in.at[e, b], rx_s.at[e, i], rx_r.at[e, i], dev(z, to, c, y))
             copy.start()
             rx.append(copy)
+
+    for d, hops in far:
+        origin = y + d
+        arrived(w_all.at[mod(y + origin + yn, yn)], wy_r.at[-d % yn])
+        for hop in hops:
+            weights(w_all.at[mod(origin + y + yn, yn)], origin, y + hop, (hop - d) % yn)
 
     def merge(all_stats, blocks):
         stats = [read_stats(block) for block in all_stats]

time: 67.7 us -> 68.8 us (1.016); the launches traced: 67.4 us -> 67.8 us
  no operation moved by 1% of the time
where the time goes in v4:
time: 68.8 us; the launch traced here: 67.8 us
  Pallas kernels  66.4 us (97%)
  local copies, waits for them, and re-layouts  1.35 us (2%)
    pallas_call x1, Pallas kernels, shards(): pl.pallas_call(kernel, name='attend_project', out_shape=jax.ShapeDtypeStr...  66.4 us

profile of v4, /device:TPU:1, one launch (start us, length us, event | category | flops | bytes accessed | tf_op | source)
XLA Modules:
  0.0 67.8 jit_solution(10776123305870098379)
XLA Ops:
  0.0 66.4 %attend_project.1 = bf16[96,128]{1,0:T(8,128)(2,1)} custom-call(bf16[16,768]{1,0:T(8,128)(2,1)} %q_ref.1, bf16[1024,768]{1,0:T(8,128)(2,1)} %k_ref.1, bf16[1024,768]{1,0:T(8,128)(2,1)} %v_ref.1, s32[8,16]{1,0:T(8,128)} %pat_ref.1, bf16[96,768]{1,0:T(8,128)(2,1)} %bitcast.3), custom_call_target="tpu_custom_call" | custom-call | flops 3000000000 | bytes 4000000 | tf_op jit(solution)/shard_map/attend_project/pallas_call | solution.py:499
  66.4 1.3 %copy.7 = bf16[128,96]{0,1:T(8,128)(2,1)} copy(bf16[128,96]{0,1:T(8,128)(2,1)} %bitcast.2) | data formatting | bytes 49152
